TPU v7x, 128 devices: a whole 4x4x4 slice. The times are simulated.
128 devices in a mesh: group: 4 (over y), dom: 32 (over z, x, core).
Axes of the slice: x: 4, y: 4, z: 4, core: 2. Of those that a mesh axis runs over, the one named last changes fastest.
Arguments:
- nodes: bfloat16 [262144, 128], P(('group', 'dom')), may hold values from -6 to 6
- mesh_edges: bfloat16 [1572864, 128], P(('group', 'dom')), may hold values from -6 to 6
- contact_edges: bfloat16 [16384, 64, 128], P(('group', 'dom')), may hold values from -6 to 6
- mesh_src: int32 [1572864], P(('group', 'dom')), may hold values from 0 to 2559, as said below
- halo_rows: int32 [256, 256], P(('group', 'dom')), may hold values from 0 to 2047
- send_rows: int32 [16384, 64], P(('group', 'dom')), may hold values from 0 to 2047
- partner_rows: int32 [16384, 64], P(('group', 'dom')), may hold values from 0 to 2047
- contact_counts: int32 [128, 128], replicated, may hold values from 1 to 64, as said below
- edge_first: bfloat16 [384, 128], replicated, may hold values from -0.3125 to 0.3125
- edge_second: bfloat16 [128, 128], replicated, may hold values from -0.5 to 0.5
- edge_third: bfloat16 [128, 128], replicated, may hold values from -0.5 to 0.5
- contact_first: bfloat16 [384, 128], replicated, may hold values from -0.3125 to 0.3125
- contact_second: bfloat16 [128, 128], replicated, may hold values from -0.5 to 0.5
- contact_third: bfloat16 [128, 128], replicated, may hold values from -0.5 to 0.5
- node_first: bfloat16 [384, 128], replicated, may hold values from -0.3125 to 0.3125
- node_second: bfloat16 [128, 128], replicated, may hold values from -0.5 to 0.5
- node_third: bfloat16 [128, 128], replicated, may hold values from -0.5 to 0.5
Outputs:
- new_nodes: bfloat16 [262144, 128], P(('group', 'dom'))
- new_mesh_edges: bfloat16 [1572864, 128], P(('group', 'dom'))
- new_contact_edges: bfloat16 [16384, 64, 128], P(('group', 'dom'))
Inputs may be any that keep to these rules, and one draw needn't show every extreme that they name: `mesh_src`: the source of device d's edge k (target node n = k // 6) lies in table rows 128 * (n // 128) to 128 * (n // 128) + 128 + 2 * 256 - 1. `contact_counts`: every device sends exactly 64 to some device, and some device receives exactly 64 from every device.
All inputs are finite; a program needn't handle non-finite values.
Results may differ from a plain program's by a relative error of at most 0.0058.
Values may be sent and summed in bfloat16 or wider, within the bound.
No kernel may reach another device: no remote copies, remote signals or barrier semaphores. Data moves between devices by JAX's collectives and lax.ppermute only.
A program may use at most 128 MiB of HBM per device.

v0:
```python
import math

import jax
import jax.numpy as jnp
from jax import lax
from jax.sharding import PartitionSpec as P

BLOCK = 128


def extended_2(block, sides, width):
    for axis, dim in sides:
        count = lax.axis_size(axis)
        forward = [(i, i + 1) for i in range(count - 1)]
        backward = [(target, source) for source, target in forward]
        low = lax.ppermute(
            lax.slice_in_dim(block, block.shape[dim] - width, None, axis=dim), axis, forward
        )
        high = lax.ppermute(lax.slice_in_dim(block, 0, width, axis=dim), axis, backward)
        block = jnp.concatenate([low, block, high], axis=dim)
    return block


def perceptron(members, first, second, third):
    feature_span = members[0].shape[-1]
    summed = jnp.zeros((members[0].shape[0], first.shape[1]), jnp.float32)
    for position, member in enumerate(members):
        summed = summed + jnp.dot(
            member,
            first[position * feature_span : (position + 1) * feature_span],
            preferred_element_type=jnp.float32,
        )
    hidden_one = jax.nn.relu(summed).astype(jnp.bfloat16)
    hidden_two = jax.nn.relu(
        jnp.dot(hidden_one, second, preferred_element_type=jnp.float32)
    ).astype(jnp.bfloat16)
    output = jnp.dot(hidden_two, third, preferred_element_type=jnp.float32)
    centred = output - jnp.mean(output, axis=-1, keepdims=True)
    return centred * lax.rsqrt(jnp.mean(centred * centred, axis=-1, keepdims=True) + 1e-05)


def pick_rows(source, row_list, row_block):
    columns = jnp.arange(source.shape[0], dtype=jnp.int32)

    def select(piece):
        selector = (piece[:, None] == columns[None, :]).astype(source.dtype)
        return jnp.dot(selector, source, preferred_element_type=jnp.float32).astype(source.dtype)

    picked = lax.map(select, row_list.reshape(-1, row_block))
    return picked.reshape(row_list.shape[0], source.shape[1])


def add_rows(values, row_list, span, row_block):
    columns = jnp.arange(span, dtype=jnp.int32)
    features = values.shape[1]

    def accumulate(total, packed):
        piece_rows, piece_values = packed
        selector = (piece_rows[:, None] == columns[None, :]).astype(jnp.bfloat16)
        term = lax.dot_general(
            selector, piece_values, (((0,), (0,)), ((), ())), preferred_element_type=jnp.float32
        )
        return (total + term, None)

    start = jnp.zeros((span, features), jnp.float32)
    total, unused = lax.scan(
        accumulate,
        start,
        (row_list.reshape(-1, row_block), values.reshape(-1, row_block, features)),
    )
    return total


def shards(
    nodes,
    mesh_edges,
    contact_edges,
    mesh_src,
    halo_rows,
    send_rows,
    partner_rows,
    contact_counts,
    edge_first,
    edge_second,
    edge_third,
    contact_first,
    contact_second,
    contact_third,
    node_first,
    node_second,
    node_third,
):
    node_count, features = nodes.shape
    seam_width = halo_rows.shape[1]
    degree = mesh_edges.shape[0] // node_count
    rim_list = halo_rows.reshape(-1)
    rim_rows = pick_rows(nodes, rim_list, rim_list.shape[0])
    extended = extended_2(rim_rows, (("dom", 0),), seam_width)
    table = jnp.concatenate([extended[:seam_width], nodes, extended[-seam_width:]], axis=0)
    block_count = node_count // BLOCK
    window_span = BLOCK + 2 * seam_width
    starts = jnp.arange(block_count, dtype=jnp.int32) * BLOCK
    windows = jax.vmap(
        lambda first_row: lax.dynamic_slice_in_dim(table, first_row, window_span, 0)
    )(starts)
    local_source = mesh_src.reshape(block_count, degree * BLOCK) - starts[:, None]
    window_index = jnp.arange(window_span, dtype=jnp.int32)
    selector = (local_source[:, :, None] == window_index[None, None, :]).astype(jnp.bfloat16)
    source_latent = (
        jnp.einsum("bew,bwf->bef", selector, windows, preferred_element_type=jnp.float32)
        .astype(jnp.bfloat16)
        .reshape(-1, features)
    )
    target_latent = jnp.broadcast_to(nodes[:, None, :], (node_count, degree, features)).reshape(
        -1, features
    )
    mesh_update = perceptron(
        (mesh_edges, source_latent, target_latent), edge_first, edge_second, edge_third
    )
    new_mesh = (mesh_edges.astype(jnp.float32) + mesh_update).astype(jnp.bfloat16)
    mesh_total = jnp.sum(
        new_mesh.astype(jnp.float32).reshape(node_count, degree, features), axis=1
    ).astype(jnp.bfloat16)
    peers, capacity = send_rows.shape
    slot_total = peers * capacity
    slot_block = math.gcd(512, slot_total)
    device_index = lax.axis_index("group") * lax.axis_size("dom") + lax.axis_index("dom")
    received_counts = lax.dynamic_index_in_dim(contact_counts, device_index, 1, keepdims=False)
    slot_index = jnp.arange(capacity, dtype=jnp.int32)
    valid_flat = (slot_index[None, :] < received_counts[:, None]).reshape(slot_total, 1)
    send_flat = send_rows.reshape(-1)
    outgoing = pick_rows(nodes, send_flat, slot_block).reshape(peers, capacity, features)
    arrived = lax.all_to_all(outgoing, ("group", "dom"), split_axis=0, concat_axis=0, tiled=True)
    partner_flat = partner_rows.reshape(-1)
    partner_latent = pick_rows(nodes, partner_flat, slot_block)
    flat_edges = contact_edges.reshape(slot_total, features)
    contact_update = perceptron(
        (flat_edges, arrived.reshape(slot_total, features), partner_latent),
        contact_first,
        contact_second,
        contact_third,
    )
    updated = (flat_edges.astype(jnp.float32) + contact_update).astype(jnp.bfloat16)
    new_contacts = jnp.where(valid_flat, updated, flat_edges)
    message = jnp.where(valid_flat, updated, jnp.zeros_like(updated))
    returned = lax.all_to_all(
        message.reshape(peers, capacity, features),
        ("group", "dom"),
        split_axis=0,
        concat_axis=0,
        tiled=True,
    ).reshape(slot_total, features)
    both_values = jnp.concatenate([message, returned], axis=0)
    both_rows = jnp.concatenate([partner_flat, send_flat], axis=0)
    world_total = add_rows(both_values, both_rows, node_count, slot_block).astype(jnp.bfloat16)
    node_update = perceptron((nodes, mesh_total, world_total), node_first, node_second, node_third)
    new_nodes = (nodes.astype(jnp.float32) + node_update).astype(jnp.bfloat16)
    return (new_nodes, new_mesh, new_contacts.reshape(peers, capacity, features))


def solution(mesh):
    in_specs = (
        P(("group", "dom"), None),
        P(("group", "dom"), None),
        P(("group", "dom"), None, None),
        P(("group", "dom")),
        P(("group", "dom"), None),
        P(("group", "dom"), None),
        P(("group", "dom"), None),
        P(),
        P(),
        P(),
        P(),
        P(),
        P(),
        P(),
        P(),
        P(),
        P(),
    )
    out_specs = (
        P(("group", "dom"), None),
        P(("group", "dom"), None),
        P(("group", "dom"), None, None),
    )
    return jax.shard_map(shards, mesh=mesh, in_specs=in_specs, out_specs=out_specs, check_vma=False)
```

profile of v0, /device:TPU:1, one launch (start us, length us, event | category | flops | bytes accessed | tf_op | source)
XLA Modules:
  0.0 345.0 jit_solution(14023653721601010908)
XLA Ops:
  4.0 3.3 collective-permute-start.1
  7.3 3.1 collective-permute-start
  13.1 24.2 %while.39 = (s32[]{:T(128)}, bf16[16,512,128]{2,1,0:T(8,128)(2,1)}, s32[16,512]{1,0:T(8,128)S(1)}, bf16[2048,128]{1,0:T(8,128)(2,1)S(1)}, s32[]{:T(128)}) while((s32[]{:T(128)}, bf16[16,512,128]{2,1,0:T(8,128)(2,1)}, s32[16,512]{1,0:T(8,128)S(1)}, bf16[2048,128]{1,0:T(8,128)(2,1)S(1)}, s32[]{:T(128)}) %tuple.90), condition=%wide.region_4.5_spmd.clone, body=%wide.region_3.4_spmd.clone.sunk | while | flops 269549568 | bytes 661581 | solution.py:49
  37.3 12.2 %all-to-all-start = ((bf16[128,64,128]{2,1,0:T(8,128)(2,1)}), bf16[128,64,128]{2,1,0:T(8,128)(2,1)}, u32[]{:S(2)}, u32[]{:S(2)}) async-start(bf16[128,64,128]{2,1,0:T(8,128)(2,1)} %bitcast.2), calls=%async_computation | async-start | bytes 4194304 | tf_op jit(solution)/shard_map/all_to_all | solution.py:133
  54.8 6.5 %reshape.155 = bf16[12288,128]{1,0:T(8,128)(2,1)} reshape(bf16[2048,6,128]{2,1,0:T(8,128)(2,1)} %broadcast_in_dim.32) | data formatting | bytes 6291456 | tf_op jit(solution)/shard_map/reshape | solution.py:114
  63.6 40.8 %while.40 = (s32[]{:T(128)}, bf16[16,512,128]{2,1,0:T(8,128)(2,1)}, s32[16,512]{1,0:T(8,128)S(1)}, bf16[2048,128]{1,0:T(8,128)(2,1)}, s32[]{:T(128)}) while((s32[]{:T(128)}, bf16[16,512,128]{2,1,0:T(8,128)(2,1)}, s32[16,512]{1,0:T(8,128)S(1)}, bf16[2048,128]{1,0:T(8,128)(2,1)}, s32[]{:T(128)}) %tuple.84), condition=%wide.region_6.7_spmd.clone, body=%wide.region_5.6_spmd.clone.sunk | while | flops 269549568 | bytes 661581 | solution.py:49
  104.5 3.6 %fusion.52 = f32[12288,128]{1,0:T(8,128)} fusion(bf16[12288,128]{1,0:T(8,128)(2,1)S(1)} %copy-done.3, bf16[384,128]{1,0:T(8,128)(2,1)S(1)} %copy-done.12), kind=kOutput, calls=%fused_computation.80 | convolution fusion | flops 402653184 | bytes 9469952 | tf_op jit(solution)/shard_map/dot_general | solution.py:28
  108.2 2.7 fusion.47
  112.5 33.2 %while.38 = (s32[]{:T(128)}, bf16[2560,128]{1,0:T(8,128)(2,1)S(1)}, s32[16,2]{0,1:T(2,128)S(1)}, bf16[16,640,128]{2,1,0:T(8,128)(2,1)}, s32[]{:T(128)}) while((s32[]{:T(128)}, bf16[2560,128]{1,0:T(8,128)(2,1)S(1)}, s32[16,2]{0,1:T(2,128)S(1)}, bf16[16,640,128]{2,1,0:T(8,128)(2,1)}, s32[]{:T(128)}) %tuple.78), condition=%wide.while_cond, body=%wide.while_body.sunk | while | flops 2 | bytes 328293 | solution.py:104
  145.7 7.3 %fusion.34 = bf16[16,768,128]{2,1,0:T(8,128)(2,1)S(1)} fusion(bf16[16,640,128]{2,1,0:T(8,128)(2,1)} %get-tuple-element.109, s32[16,768]{1,0:T(8,128)S(1)} %broadcast_subtract_fusion), kind=kOutput, calls=%fused_computation.55 | convolution fusion | flops 2022703104 | bytes 5816320 | tf_op jit(solution)/shard_map/bew,bwf->bef/dot_general | solution.py:110
  156.0 4.6 %fusion.60 = (f32[12288]{0:T(1024)S(1)}, f32[12288,128]{1,0:T(8,128)}) fusion(bf16[128,128]{1,0:T(8,128)(2,1)S(1)} %copy-done.16, bf16[12288,128]{1,0:T(8,128)(2,1)S(1)} %fusion.26, bf16[128,128]{1,0:T(8,128)(2,1)S(1)} %copy-done.17), kind=kOutput, calls=%fused_computation.95 | convolution fusion | flops 810012672 | bytes 9551872 | tf_op jit(solution)/shard_map/dot_general | solution.py:37
  160.5 5.7 %multiply_reduce_fusion = f32[12288]{0:T(1024)S(1)} fusion(f32[12288,128]{1,0:T(8,128)} %get-tuple-element.190, f32[12288]{0:T(1024)S(1)} %broadcast_multiply_fusion), kind=kLoop, calls=%fused_computation.43 | loop fusion | flops 4706304 | bytes 6389760 | tf_op jit(solution)/shard_map/reduce_sum | solution.py:39
  166.3 5.6 %convolution_add_fusion.3 = f32[8192,128]{1,0:T(8,128)} fusion(f32[8192,128]{1,0:T(8,128)} %fusion.47, bf16[8192,128]{1,0:T(8,128)(2,1)} %bitcast.3, bf16[384,128]{1,0:T(8,128)(2,1)S(1)} %copy-done.13), kind=kOutput, calls=%fused_computation.39 | convolution fusion | flops 269484032 | bytes 10518528 | tf_op jit(solution)/shard_map/dot_general | solution.py:28
  171.9 4.2 %fusion.28 = bf16[8192,128]{1,0:T(8,128)(2,1)S(1)} fusion(bf16[128,128]{1,0:T(8,128)(2,1)S(1)} %copy-done.18, f32[8192,128]{1,0:T(8,128)} %convolution_add_fusion.3, bf16[8192,128]{1,0:T(8,128)(2,1)} %bitcast.79, bf16[384,128]{1,0:T(8,128)(2,1)S(1)} %copy-done.13), kind=kOutput, calls=%fused_computation.40 | convolution fusion | flops 542113792 | bytes 8454144 | tf_op jit(solution)/shard_map/dot_general | solution.py:35
  179.9 7.9 %broadcast_select_fusion = (bf16[8192,128]{1,0:T(8,128)(2,1)}, bf16[8192,128]{1,0:T(8,128)(2,1)}) fusion(pred[8192]{0:T(1024)(128)(4,1)S(1)} %lt.52, bf16[128,64,128]{2,1,0:T(8,128)(2,1)S(1)} %copy-done.6, f32[8192]{0:T(1024)S(1)} %add_rsqrt_fusion.1, f32[8192,128]{1,0:T(8,128)S(1)} %get-tuple-element.192, f32[8192]{0:T(1024)S(1)} %broadcast_multiply_fusion.1), kind=kLoop, calls=%fused_computation.58 | loop fusion | flops 7340032 | bytes 10559488 | tf_op jit(solution)/shard_map/jit(_where)/select_n | solution.py:144
  187.8 10.2 %all-to-all-start.1 = ((bf16[128,64,128]{2,1,0:T(8,128)(2,1)}), bf16[128,64,128]{2,1,0:T(8,128)(2,1)}, u32[]{:S(2)}, u32[]{:S(2)}) async-start(bf16[128,64,128]{2,1,0:T(8,128)(2,1)} %bitcast.5), calls=%async_computation.1 | async-start | bytes 4194304 | tf_op jit(solution)/shard_map/all_to_all | solution.py:146
  198.0 10.0 %add_convert_fusion = bf16[12288,128]{1,0:T(8,128)(2,1)} fusion(bf16[12288,128]{1,0:T(8,128)(2,1)S(1)} %copy-done.4, f32[12288,128]{1,0:T(8,128)} %get-tuple-element.190, f32[12288]{0:T(1024)S(1)} %add_rsqrt_fusion, f32[12288]{0:T(1024)S(1)} %broadcast_multiply_fusion), kind=kLoop, calls=%fused_computation.42 | loop fusion | flops 7864320 | bytes 12681216 | tf_op jit(solution)/shard_map/convert_element_type | solution.py:120
  208.0 6.3 %reshape.156 = bf16[2048,6,128]{2,1,0:T(8,128)(2,1)} reshape(bf16[12288,128]{1,0:T(8,128)(2,1)} %add_convert_fusion) | data formatting | bytes 6291456 | tf_op jit(solution)/shard_map/reshape | solution.py:122
  214.3 12.5 %reduce = bf16[2048,128]{1,0:T(8,128)(2,1)S(1)} reduce(bf16[2048,6,128]{2,1,0:T(8,128)(2,1)} %reshape.156, bf16[]{:T(256)} %constant.85.clone.1), dimensions={1}, to_apply=%region_2.3.clone | reduce | flops 1310720 | bytes 3670018 | tf_op jit(solution)/shard_map/reduce_sum | solution.py:121
  228.2 5.7 %pad_maximum_fusion = bf16[16384,128]{1,0:T(8,128)(2,1)} fusion(bf16[8192,128]{1,0:T(8,128)(2,1)} %bitcast.6, bf16[8192,128]{1,0:T(8,128)(2,1)} %get-tuple-element.186), kind=kLoop, calls=%fused_computation.44 | loop fusion | flops 8388608 | bytes 8388608 | tf_op jit(solution)/shard_map/concatenate | solution.py:153
  233.9 108.9 %while.41 = (s32[]{:T(128)}, f32[2048,128]{1,0:T(8,128)S(1)}, s32[32,512]{1,0:T(8,128)}, bf16[32,512,128]{2,1,0:T(8,128)(2,1)}, s32[]{:T(128)}, /*index=5*/s32[]{:T(128)}) while((s32[]{:T(128)}, f32[2048,128]{1,0:T(8,128)S(1)}, s32[32,512]{1,0:T(8,128)}, bf16[32,512,128]{2,1,0:T(8,128)(2,1)}, s32[]{:T(128)}, ...), condition=%wide.region_10.11_spmd.clone, body=%wide.region_9.10_spmd.clone.sunk | while | flops 270008320 | bytes 2234463 | solution.py:66
  234.6 2.7 fusion.95
  238.0 2.7 fusion.95
  241.4 2.7 fusion.95
  244.8 2.7 fusion.95
  248.2 2.7 fusion.95
  251.6 2.7 fusion.95
  255.0 2.7 fusion.95
  258.4 2.7 fusion.95
  261.9 2.7 fusion.95
  265.3 2.7 fusion.95
  268.7 2.7 fusion.95
  272.1 2.7 fusion.95
  275.5 2.7 fusion.95
  278.9 2.7 fusion.95
  282.3 2.7 fusion.95
  285.7 2.7 fusion.95
  289.1 2.7 fusion.95
  292.5 2.7 fusion.95
  295.9 2.7 fusion.95
  299.3 2.7 fusion.95
  306.1 2.7 fusion.95
  309.5 2.7 fusion.95
  316.3 2.7 fusion.95
  319.7 2.7 fusion.95
  323.1 2.7 fusion.95
  329.9 2.7 fusion.95
  333.3 2.7 fusion.95
  (244 shorter events, 160.0 us)
Async XLA Ops:
  0.6 60.9 %copy-start = (s32[128,128]{1,0:T(8,128)S(1)}, s32[128,128]{1,0:T(8,128)}, u32[]{:S(2)}) copy-start(s32[128,128]{1,0:T(8,128)} %param.30) | copy-start | bytes 196612
  0.6 12.4 %copy-start.7 = (bf16[2048,128]{1,0:T(8,128)(2,1)S(1)}, bf16[2048,128]{1,0:T(8,128)(2,1)}, u32[]{:S(2)}) copy-start(bf16[2048,128]{1,0:T(8,128)(2,1)} %param.23) | copy-start | bytes 1572868
  4.0 107.6 %collective-permute-start.1 = (bf16[256,128]{1,0:T(8,128)(2,1)}, bf16[256,128]{1,0:T(8,128)(2,1)}, u32[]{:S(2)}, u32[]{:S(2)}) collective-permute-start(bf16[256,128]{1,0:T(8,128)(2,1)} %get-tuple-element.188), channel_id=1, source_target_pairs={{1,0},{2,1},{3,2},{4,3},{5,4},{6,5},{7,6},{8,7},{9,8},{10,9},{11,1... | collective-permute-start | bytes 196616 | tf_op jit(solution)/shard_map/ppermute | solution.py:19
  7.3 104.3 %collective-permute-start = (bf16[256,128]{1,0:T(8,128)(2,1)}, bf16[256,128]{1,0:T(8,128)(2,1)}, u32[]{:S(2)}, u32[]{:S(2)}) collective-permute-start(bf16[256,128]{1,0:T(8,128)(2,1)} %get-tuple-element.187), channel_id=1, source_target_pairs={{0,1},{1,2},{2,3},{3,4},{4,5},{5,6},{6,7},{7,8},{8,9},{9,10},{10,1... | collective-permute-start | bytes 196616 | tf_op jit(solution)/shard_map/ppermute | solution.py:16
  37.3 15.3 %copy-start.15 = (s32[12288]{0:T(1024)S(1)}, s32[12288]{0:T(1024)}, u32[]{:S(2)}) copy-start(s32[12288]{0:T(1024)} %param.26) | copy-start | bytes 147460
  37.3 129.0 %all-to-all-start = ((bf16[128,64,128]{2,1,0:T(8,128)(2,1)}), bf16[128,64,128]{2,1,0:T(8,128)(2,1)}, u32[]{:S(2)}, u32[]{:S(2)}) async-start(bf16[128,64,128]{2,1,0:T(8,128)(2,1)} %bitcast.2), calls=%async_computation | async-start | bytes 4194304 | tf_op jit(solution)/shard_map/all_to_all | solution.py:133
  54.8 6.5 %copy-start.21 = (s32[128,64]{0,1:T(8,128)S(1)}, s32[128,64]{0,1:T(8,128)}, u32[]{:S(2)}) copy-start(s32[128,64]{0,1:T(8,128)} %param.29) | copy-start | bytes 98308
  61.9 42.6 %copy-start.3 = (bf16[12288,128]{1,0:T(8,128)(2,1)S(1)}, bf16[12288,128]{1,0:T(8,128)(2,1)}, u32[]{:S(2)}) copy-start(bf16[12288,128]{1,0:T(8,128)(2,1)} %param.24) | copy-start | bytes 9437188
  63.6 40.8 %copy-start.12 = (bf16[384,128]{1,0:T(8,128)(2,1)S(1)}, bf16[384,128]{1,0:T(8,128)(2,1)}, u32[]{:S(2)}) copy-start(bf16[384,128]{1,0:T(8,128)(2,1)} %param.31) | copy-start | bytes 294916
  104.4 3.7 %copy-start.5 = (bf16[128,64,128]{2,1,0:T(8,128)(2,1)S(1)}, bf16[128,64,128]{2,1,0:T(8,128)(2,1)}, u32[]{:S(2)}) copy-start(bf16[128,64,128]{2,1,0:T(8,128)(2,1)} %param.25) | copy-start | bytes 6291460
  104.4 3.7 %copy-start.13 = (bf16[384,128]{1,0:T(8,128)(2,1)S(1)}, bf16[384,128]{1,0:T(8,128)(2,1)}, u32[]{:S(2)}) copy-start(bf16[384,128]{1,0:T(8,128)(2,1)} %param.34) | copy-start | bytes 294916
  108.2 3.4 copy-start.8
  112.5 40.6 %slice-start = ((s8[6291456]{0:T(1024)(128)(4,1)}), s8[2097152]{0:T(1024)(128)(4,1)S(1)}, s32[]{:S(2)}) async-start(s8[6291456]{0:T(1024)(128)(4,1)} %bitcast.75), calls=%async_computation.2 | async-start | bytes 4194304
  145.7 7.4 %slice-start.1 = ((s8[6291456]{0:T(1024)(128)(4,1)}), s8[4194304]{0:T(1024)(128)(4,1)S(1)}, s32[]{:S(2)}) async-start(s8[6291456]{0:T(1024)(128)(4,1)} %bitcast.75), calls=%async_computation.3 | async-start | bytes 8388608
  153.1 1.9 copy-start.2
  155.0 1.0 copy-start.16
  155.0 1.0 copy-start.17
  166.3 5.6 %copy-start.18 = (bf16[128,128]{1,0:T(8,128)(2,1)S(1)}, bf16[128,128]{1,0:T(8,128)(2,1)}, u32[]{:S(2)}) copy-start(bf16[128,128]{1,0:T(8,128)(2,1)} %param.35) | copy-start | bytes 98308
  171.9 4.2 %copy-start.19 = (bf16[128,128]{1,0:T(8,128)(2,1)S(1)}, bf16[128,128]{1,0:T(8,128)(2,1)}, u32[]{:S(2)}) copy-start(bf16[128,128]{1,0:T(8,128)(2,1)} %param.36) | copy-start | bytes 98308
  177.4 2.4 copy-start.6
  187.8 10.2 %copy-start.4 = (bf16[12288,128]{1,0:T(8,128)(2,1)S(1)}, bf16[12288,128]{1,0:T(8,128)(2,1)}, u32[]{:S(2)}) copy-start(bf16[12288,128]{1,0:T(8,128)(2,1)} %param.24) | copy-start | bytes 9437188
  187.8 40.4 %all-to-all-start.1 = ((bf16[128,64,128]{2,1,0:T(8,128)(2,1)}), bf16[128,64,128]{2,1,0:T(8,128)(2,1)}, u32[]{:S(2)}, u32[]{:S(2)}) async-start(bf16[128,64,128]{2,1,0:T(8,128)(2,1)} %bitcast.5), calls=%async_computation.1 | async-start | bytes 4194304 | tf_op jit(solution)/shard_map/all_to_all | solution.py:146
  214.3 12.6 %copy-start.9 = (f32[2048,128]{1,0:T(8,128)S(1)}, f32[2048,128]{1,0:T(8,128)}, u32[]{:S(2)}) copy-start(f32[2048,128]{1,0:T(8,128)} %fusion.54) | copy-start | bytes 3145732
  214.3 12.6 %copy-start.14 = (bf16[384,128]{1,0:T(8,128)(2,1)S(1)}, bf16[384,128]{1,0:T(8,128)(2,1)}, u32[]{:S(2)}) copy-start(bf16[384,128]{1,0:T(8,128)(2,1)} %param.37) | copy-start | bytes 294916
  228.2 5.7 %copy-start.11 = (f32[2048,128]{1,0:T(8,128)S(1)}, f32[2048,128]{1,0:T(8,128)}, u32[]{:S(2)}) copy-start(f32[2048,128]{1,0:T(8,128)} %custom-call) | copy-start | bytes 3145732
  233.9 108.9 %copy-start.20 = (bf16[128,128]{1,0:T(8,128)(2,1)S(1)}, bf16[128,128]{1,0:T(8,128)(2,1)}, u32[]{:S(2)}) copy-start(bf16[128,128]{1,0:T(8,128)(2,1)} %param.38) | copy-start | bytes 98308
  233.9 109.5 %copy-start.22 = (bf16[128,128]{1,0:T(8,128)(2,1)S(1)}, bf16[128,128]{1,0:T(8,128)(2,1)}, u32[]{:S(2)}) copy-start(bf16[128,128]{1,0:T(8,128)(2,1)} %param.39) | copy-start | bytes 98308
  342.8 1.1 copy-start.10
  342.8 2.3 copy-start.1
where the time goes:
time: 349 us; the launch traced here: 345 us
  matrix products  186 us (53%)
  local copies, waits for them, and re-layouts  81 us (23%)
  other arithmetic  46.4 us (13%)
  starting transfers between devices  28.9 us (8%)
    dot_general x32, matrix products, accumulate(): lax.dot_general(selector, piece_values, (((0,), (0,)), ((), ())), preferr...  84.9 us
    dot_general x33, matrix products, select(): jnp.dot(selector, source, preferred_element_type=jnp.float32)  66.7 us
    gather x48, local copies, waits for them, and re-layouts  33.2 us
    dynamic_slice x32, local copies, waits for them, and re-layouts, add_rows(): lax.scan(accumulate, start, (row_list.reshape(-1, row_block), values.resh...  23.3 us
    dot_general x7, matrix products, perceptron(): jnp.dot(member, first[position * feature_span:(position + 1) * feature_sp...  16.2 us
    reduce_sum x1, other arithmetic, shards(): jnp.sum(new_mesh.astype(jnp.float32).reshape(node_count, degree, features...  12.5 us
    all_to_all x1, starting transfers between devices, shards(): lax.all_to_all(outgoing, ('group', 'dom'), split_axis=0, concat_axis=0, t...  12.2 us
    all_to_all x1, starting transfers between devices, shards(): lax.all_to_all(message.reshape(peers, capacity, features), ('group', 'dom...  10.2 us
  transfers between devices with their start and end apart: 4, of which 1 were waited for; matrix products, arithmetic and copies ran while one was open for 50% of the time, Pallas kernels for 0%

commit v1 on v0

v1 whole, which is shorter than its diff:
```python
import functools

import jax
import jax.numpy as jnp
from jax import lax
from jax.experimental import pallas as pl
from jax.experimental.pallas import tpu as pltpu
from jax.sharding import PartitionSpec as P

W = 128
BLOCK = 128
HALO = 256
SPLIT = 2
F32 = jnp.float32
BF16 = jnp.bfloat16
ANY = pl.BlockSpec(memory_space=pl.ANY)


def dot(a, b):
    return jnp.dot(a, b, preferred_element_type=F32)


def params(mib=60):
    return pltpu.CompilerParams(vmem_limit_bytes=mib << 20)


def whole(shape):
    return pl.BlockSpec(shape, lambda i: (0,) * len(shape))


def pair(x):
    half = x.shape[0] // 2
    return jnp.concatenate([x[:half], x[half:]], axis=1)


def unpair(x):
    return jnp.concatenate([x[:, :W], x[:, W:]], axis=0)


def twice(w):
    zero = jnp.zeros_like(w)
    return jnp.concatenate(
        [jnp.concatenate([w, zero], axis=1), jnp.concatenate([zero, w], axis=1)], axis=0
    )


def centre(w):
    wide = w.astype(F32)
    wide = wide - jnp.mean(wide, axis=1, keepdims=True)
    high = wide.astype(BF16)
    return high, (wide - high.astype(F32)).astype(BF16)


def fill(weights_ref, second, third):
    weights_ref[0] = twice(second)
    high, low = centre(third)
    weights_ref[1] = twice(high)
    weights_ref[2] = twice(low)
    weights_ref[3] = twice(jnp.full((W, W), 1.0 / W, BF16))


def tail(summed, weights_ref):
    one = jnp.maximum(summed, 0.0).astype(BF16)
    two = jnp.maximum(dot(one, weights_ref[0]), 0.0).astype(BF16)
    centred = dot(two, weights_ref[1]) + dot(two, weights_ref[2])
    variance = dot((centred * centred).astype(BF16), weights_ref[3])
    return centred * lax.rsqrt(variance + 1e-05)


def columns(rows):
    count, length = rows.shape
    return jnp.concatenate(
        [jnp.broadcast_to(rows[i : i + 1], (W, length)).T for i in range(count)], axis=0
    )


def columns_down(rows_ref, peers):
    rows = rows_ref[...]
    steps = rows.shape[1] // peers
    if steps > 1:
        rows = pltpu.roll(rows, (steps - pl.program_id(0)) % steps * peers, 1)
    return jnp.concatenate(
        [jnp.broadcast_to(rows[:, i : i + 1], (rows.shape[0], W)) for i in range(peers)], axis=0
    )


def one_hot(column, span):
    lane = lax.broadcasted_iota(jnp.int32, (column.shape[0], W), 1).astype(jnp.int16)
    short = column.astype(jnp.int16)
    one, zero = jnp.ones((), BF16), jnp.zeros((), BF16)
    return jnp.concatenate(
        [
            jnp.where(short == lane + jnp.int16(first), one, zero)
            for first in range(0, span, W)
        ],
        axis=1,
    )


def one_hot_down(row, first, height):
    index = lax.broadcasted_iota(jnp.int32, (height, row.shape[1]), 0) + first
    wide = jnp.broadcast_to(row, index.shape)
    return jnp.where(
        wide.astype(jnp.int16) == index.astype(jnp.int16), jnp.ones((), BF16), jnp.zeros((), BF16)
    )


def picked(column, nodes_ref, split=SPLIT):
    span = nodes_ref.shape[0] // split
    table = jnp.concatenate([nodes_ref[r * span : (r + 1) * span] for r in range(split)], axis=1)
    result = dot(one_hot(column & (span - 1), span), table)
    part = column >> (span.bit_length() - 1)
    out = result[:, :W]
    for r in range(1, split):
        out = jnp.where(part == r, result[:, r * W : (r + 1) * W], out)
    return out.astype(BF16)


def gather_kernel(peers, rows_ref, nodes_ref, out_ref):
    out_ref[...] = picked(columns_down(rows_ref, peers), nodes_ref)


def gather_rows(rows, nodes, peers):
    length, count = rows.shape
    return pl.pallas_call(
        functools.partial(gather_kernel, peers),
        grid=(count // peers,),
        in_specs=[whole(rows.shape), whole(nodes.shape)],
        out_specs=pl.BlockSpec((peers * length, W), lambda i: (i, 0)),
        out_shape=jax.ShapeDtypeStruct((count * length, W), BF16),
        compiler_params=params(),
        cost_estimate=pl.CostEstimate(
            flops=2 * count * length * nodes.shape[0] * W,
            bytes_accessed=count * length * W * 2,
            transcendentals=0,
        ),
    )(rows, nodes)


def rim_kernel(rows_ref, nodes_ref, out_ref):
    out_ref[...] = picked(columns(rows_ref[...]), nodes_ref)


def rim_rows(rows, nodes):
    return pl.pallas_call(
        rim_kernel,
        out_shape=jax.ShapeDtypeStruct((rows.size, W), BF16),
        compiler_params=params(),
        cost_estimate=pl.CostEstimate(
            flops=2 * rows.size * nodes.shape[0] * W,
            bytes_accessed=(rows.size + nodes.shape[0]) * W * 2,
            transcendentals=0,
        ),
    )(rows, nodes)


def partner_kernel(peers, rows_ref, nodes_ref, edges_ref, first_ref, out_ref):
    latent = picked(columns_down(rows_ref, peers), nodes_ref)
    weights = jnp.concatenate([first_ref[:W], first_ref[2 * W :]], axis=0)
    out_ref[...] = dot(jnp.concatenate([edges_ref[...], latent], axis=1), weights)


def partner_part(rows, nodes, edges, first, peers):
    length, count = rows.shape
    return pl.pallas_call(
        functools.partial(partner_kernel, peers),
        grid=(count // peers,),
        in_specs=[
            whole(rows.shape),
            whole(nodes.shape),
            pl.BlockSpec((peers * length, W), lambda i: (i, 0)),
            whole(first.shape),
        ],
        out_specs=pl.BlockSpec((peers * length, W), lambda i: (i, 0)),
        out_shape=jax.ShapeDtypeStruct((count * length, W), F32),
        compiler_params=params(),
        cost_estimate=pl.CostEstimate(
            flops=2 * count * length * (nodes.shape[0] + 2 * W) * W,
            bytes_accessed=count * length * W * 8,
            transcendentals=0,
        ),
    )(rows, nodes, edges, first)


def contact_kernel(
    capacity, counts_ref, arrived_ref, part_ref, edges_ref, first_ref, second_ref, third_ref,
    after_ref, new_ref, message_ref, entry_ref, weights_ref,
):
    @pl.when(pl.program_id(0) == 0)
    def prepare():
        entry_ref[...] = twice(first_ref[W : 2 * W])
        fill(weights_ref, second_ref[...], third_ref[...])

    rows = arrived_ref.shape[0]
    peers = rows // capacity
    summed = pair(part_ref[...]) + dot(pair(arrived_ref[...]), entry_ref[...])
    update = unpair(tail(summed, weights_ref))
    slot = lax.broadcasted_iota(jnp.int32, (capacity, W), 0)
    for p in range(peers):
        span = slice(p * capacity, (p + 1) * capacity)
        valid = slot < counts_ref[pl.program_id(0) * peers + p]
        old = edges_ref[span].astype(F32)
        new = old + update[span]
        new_ref[span] = jnp.where(valid, new, old).astype(BF16)
        message_ref[span] = jnp.where(valid, new, 0.0).astype(BF16)


def contact_rest(counts, arrived, part, edges, first, second, third, after, rows, capacity):
    total = arrived.shape[0]
    block = pl.BlockSpec((rows, W), lambda i, counts: (i, 0))

    def full(x):
        return pl.BlockSpec(x.shape, lambda i, counts: (0, 0))

    return pl.pallas_call(
        functools.partial(contact_kernel, capacity),
        grid_spec=pltpu.PrefetchScalarGridSpec(
            num_scalar_prefetch=1,
            grid=(total // rows,),
            in_specs=[block, block, block, full(first), full(second), full(third), ANY],
            out_specs=[block, block],
            scratch_shapes=[
                pltpu.VMEM((2 * W, 2 * W), BF16),
                pltpu.VMEM((4, 2 * W, 2 * W), BF16),
            ],
        ),
        out_shape=[jax.ShapeDtypeStruct((total, W), BF16)] * 2,
        compiler_params=params(),
        cost_estimate=pl.CostEstimate(
            flops=2 * total * 4 * W * W, bytes_accessed=total * W * 12, transcendentals=total * W
        ),
    )(counts, arrived, part, edges, first, second, third, after)


def add_messages(rows_ref, values_ref, total_ref, split=SPLIT):
    span = total_ref.shape[0]
    rows = rows_ref[...]
    shift = span.bit_length() - 1
    values = values_ref[...]
    part = columns(rows >> shift).astype(jnp.int16)
    zero = jnp.zeros((), BF16)
    wide = jnp.concatenate(
        [jnp.where(part == jnp.int16(r), values, zero) for r in range(split)], axis=1
    )
    low = rows & (span - 1)
    height = 256
    for first in range(0, span, height):
        hot = jnp.concatenate(
            [one_hot_down(low[i : i + 1], first, height) for i in range(rows.shape[0])], axis=1
        )
        total_ref[first : first + height] += dot(hot, wide)


def received_kernel(rows_ref, values_ref, total_ref):
    @pl.when(pl.program_id(0) == 0)
    def clear():
        total_ref[...] = jnp.zeros_like(total_ref)

    add_messages(rows_ref, values_ref, total_ref)


def received_sum(rows, values, node_count, step):
    shape = (node_count // SPLIT, SPLIT * W)
    return pl.pallas_call(
        received_kernel,
        grid=(rows.shape[0] // step,),
        in_specs=[
            pl.BlockSpec((step, W), lambda i: (i, 0)),
            pl.BlockSpec((step * W, W), lambda i: (i, 0)),
        ],
        out_specs=whole(shape),
        out_shape=jax.ShapeDtypeStruct(shape, F32),
        compiler_params=params(),
        cost_estimate=pl.CostEstimate(
            flops=2 * values.shape[0] * node_count * W,
            bytes_accessed=values.size * 2,
            transcendentals=0,
        ),
    )(rows, values)


def node_kernel(
    rows_ref, values_ref, received_ref, nodes_ref, mesh_ref, first_ref, second_ref, third_ref,
    out_ref, total_ref, weights_ref,
):
    @pl.when(pl.program_id(0) == 0)
    def clear():
        total_ref[...] = received_ref[...]

    add_messages(rows_ref, values_ref, total_ref)

    @pl.when(pl.program_id(0) == pl.num_programs(0) - 1)
    def finish():
        span = total_ref.shape[0]
        world = total_ref[...].astype(BF16)
        nodes = nodes_ref[...]
        mesh = mesh_ref[...]
        summed = dot(pair(nodes), twice(first_ref[:W]))
        summed += dot(pair(mesh), twice(first_ref[W : 2 * W]))
        summed += dot(world, twice(first_ref[2 * W :]))
        fill(weights_ref, second_ref[...], third_ref[...])
        update = tail(summed, weights_ref)
        out_ref[:span] = (nodes[:span].astype(F32) + update[:, :W]).astype(BF16)
        out_ref[span:] = (nodes[span:].astype(F32) + update[:, W:]).astype(BF16)


def node_update(rows, values, received, nodes, mesh_total, first, second, third, step):
    return pl.pallas_call(
        node_kernel,
        grid=(rows.shape[0] // step,),
        in_specs=[
            pl.BlockSpec((step, W), lambda i: (i, 0)),
            pl.BlockSpec((step * W, W), lambda i: (i, 0)),
            whole(received.shape),
            whole(nodes.shape),
            whole(mesh_total.shape),
            whole(first.shape),
            whole(second.shape),
            whole(third.shape),
        ],
        out_specs=whole(nodes.shape),
        out_shape=jax.ShapeDtypeStruct(nodes.shape, BF16),
        scratch_shapes=[
            pltpu.VMEM(received.shape, F32),
            pltpu.VMEM((4, 2 * W, 2 * W), BF16),
        ],
        compiler_params=params(),
        cost_estimate=pl.CostEstimate(
            flops=2 * values.shape[0] * nodes.shape[0] * W,
            bytes_accessed=values.size * 2 + nodes.size * 8,
            transcendentals=nodes.size,
        ),
    )(rows, values, received, nodes, mesh_total, first, second, third)


def mesh_block(degree, block, table_ref, offset, source_ref, edges_ref, first_ref, weights_ref):
    seam = HALO
    span = BLOCK + 2 * seam
    base_row = pl.multiple_of(block * BLOCK, BLOCK)
    edges_here = degree * BLOCK
    window = table_ref[pl.ds(pl.multiple_of(base_row - offset, BLOCK), span)]
    own = table_ref[pl.ds(pl.multiple_of(base_row - offset + seam, BLOCK), BLOCK)]
    table = jnp.concatenate(
        [
            jnp.concatenate([window, jnp.zeros_like(window)], axis=1),
            jnp.concatenate([jnp.zeros_like(own), own], axis=1),
        ],
        axis=0,
    )
    source = one_hot(columns(source_ref[0] - base_row), span)
    edge_row = lax.broadcasted_iota(jnp.int32, (edges_here, W), 0)
    base = lax.broadcasted_iota(jnp.int32, (edges_here, W), 1) * degree
    near = (edge_row >= base) & (edge_row < base + degree)
    target = jnp.where(near, 1.0, 0.0).astype(BF16)
    latent = dot(jnp.concatenate([source, target], axis=1), table).astype(BF16)
    edges = edges_ref[...]
    summed = dot(jnp.concatenate([edges, latent], axis=1), first_ref[...])
    update = unpair(tail(pair(summed), weights_ref))
    new = (edges.astype(F32) + update).astype(BF16)
    down = lax.broadcasted_iota(jnp.int32, (BLOCK, edges_here), 0) * degree
    across = lax.broadcasted_iota(jnp.int32, (BLOCK, edges_here), 1)
    hold = jnp.where((across >= down) & (across < down + degree), 1.0, 0.0).astype(BF16)
    return new, dot(hold, new).astype(BF16)


def inner_kernel(
    degree, place, source_ref, edges_ref, nodes_ref, first_ref, second_ref, third_ref, new_ref,
    total_ref, weights_ref,
):
    @pl.when(pl.program_id(0) == 0)
    def prepare():
        fill(weights_ref, second_ref[...], third_ref[...])

    new_ref[...], total_ref[...] = mesh_block(
        degree, place(pl.program_id(0)), nodes_ref, HALO, source_ref, edges_ref, first_ref,
        weights_ref,
    )


def outer_kernel(
    degree, place, source_ref, edges_ref, nodes_ref, first_ref, second_ref, third_ref, lower_ref,
    upper_ref, mesh_ref, sums_ref, after_ref, new_ref, total_ref, weights_ref, table_ref,
):
    count = nodes_ref.shape[0]

    @pl.when(pl.program_id(0) == 0)
    def prepare():
        fill(weights_ref, second_ref[...], third_ref[...])
        table_ref[:HALO] = lower_ref[...]
        table_ref[HALO : HALO + count] = nodes_ref[...]
        table_ref[HALO + count :] = upper_ref[...]

    new_ref[...], total_ref[...] = mesh_block(
        degree, place(pl.program_id(0)), table_ref, 0, source_ref, edges_ref, first_ref,
        weights_ref,
    )


def mesh_update(kernel, place, steps, source, edges, nodes, weights, extra=(), alias=False):
    degree = edges.shape[0] // nodes.shape[0]
    here = degree * BLOCK
    scratch = [pltpu.VMEM((4, 2 * W, 2 * W), BF16)]
    extra_specs = []
    if alias:
        scratch.append(pltpu.VMEM((nodes.shape[0] + 2 * HALO, W), BF16))
        extra_specs = [whole(extra[0].shape), whole(extra[1].shape), ANY, ANY, ANY]
    return pl.pallas_call(
        functools.partial(kernel, degree, place),
        grid=(steps,),
        in_specs=[
            pl.BlockSpec((1, degree, BLOCK), lambda i: (place(i), 0, 0)),
            pl.BlockSpec((here, W), lambda i: (place(i), 0)),
            whole(nodes.shape),
        ]
        + [whole(w.shape) for w in weights]
        + extra_specs,
        out_specs=[
            pl.BlockSpec((here, W), lambda i: (place(i), 0)),
            pl.BlockSpec((BLOCK, W), lambda i: (place(i), 0)),
        ],
        out_shape=[
            jax.ShapeDtypeStruct(edges.shape, BF16),
            jax.ShapeDtypeStruct(nodes.shape, BF16),
        ],
        scratch_shapes=scratch,
        input_output_aliases={8: 0, 9: 1} if alias else {},
        compiler_params=params(),
        cost_estimate=pl.CostEstimate(
            flops=2 * steps * here * 1800 * W,
            bytes_accessed=steps * here * W * 4,
            transcendentals=steps * here * W,
        ),
    )(source, edges, nodes, *weights, *extra)


def shards(
    nodes,
    mesh_edges,
    contact_edges,
    mesh_src,
    halo_rows,
    send_rows,
    partner_rows,
    contact_counts,
    edge_first,
    edge_second,
    edge_third,
    contact_first,
    contact_second,
    contact_third,
    node_first,
    node_second,
    node_third,
):
    axes = ("group", "dom")
    node_count = nodes.shape[0]
    degree = mesh_edges.shape[0] // node_count
    peers, capacity = send_rows.shape
    slots = peers * capacity

    outgoing = gather_rows(send_rows.T, nodes, 32).reshape(peers, capacity, W)
    arrived = lax.all_to_all(outgoing, axes, split_axis=0, concat_axis=0, tiled=True)

    edges = contact_edges.reshape(slots, W)
    part = partner_part(partner_rows.T, nodes, edges, contact_first, 32)
    blocks = node_count // BLOCK
    edge_blocks = HALO // BLOCK
    source = mesh_src.reshape(blocks, degree, BLOCK)
    edge_weights = (edge_first, edge_second, edge_third)
    inner_mesh, inner_total = mesh_update(
        inner_kernel, lambda i: i + edge_blocks, blocks - 2 * edge_blocks, source, mesh_edges,
        nodes, edge_weights,
    )

    size = lax.axis_size("dom")
    device = lax.axis_index("group") * size + lax.axis_index("dom")
    counts = lax.dynamic_index_in_dim(contact_counts, device, 1, keepdims=False)
    new_contacts, message = contact_rest(
        counts, arrived.reshape(slots, W), part, edges, contact_first, contact_second,
        contact_third, inner_total, 1024, capacity,
    )
    returned = lax.all_to_all(
        message.reshape(peers, capacity, W), axes, split_axis=0, concat_axis=0, tiled=True
    ).reshape(slots, W)

    rims = rim_rows(halo_rows.reshape(-1, W), nodes)
    lower = lax.ppermute(rims[HALO:], "dom", [(i, i + 1) for i in range(size - 1)])
    upper = lax.ppermute(rims[:HALO], "dom", [(i + 1, i) for i in range(size - 1)])
    new_mesh, mesh_total = mesh_update(
        outer_kernel,
        lambda i: jnp.where(i < edge_blocks, i, i + blocks - 2 * edge_blocks),
        2 * edge_blocks, source, mesh_edges, nodes, edge_weights,
        (lower, upper, inner_mesh, inner_total, message), True,
    )
    received = received_sum(partner_rows.reshape(-1, W), message, node_count, 16)
    new_nodes = node_update(
        send_rows.reshape(-1, W), returned, received, nodes, mesh_total, node_first, node_second,
        node_third, 16,
    )
    return (new_nodes, new_mesh, new_contacts.reshape(peers, capacity, W))


def solution(mesh):
    split = P(("group", "dom"))
    in_specs = (split,) * 7 + (P(),) * 10
    return jax.shard_map(
        shards, mesh=mesh, in_specs=in_specs, out_specs=(split,) * 3, check_vma=False
    )
```

time: 349 us -> 130 us (0.37); the launches traced: 345 us -> 130 us
  matrix products: 186 us -> 0 us
  Pallas kernels: 0 us -> 80 us
  local copies, waits for them, and re-layouts: 81 us -> 7.68 us
  other arithmetic: 46.4 us -> 0 us
  waiting for transfers between devices: 0.97 us -> 14.4 us
    dot_general x78 -> x0, matrix products: 186 us -> none  [the longest x32 84.9 us: accumulate(): lax.dot_general(selector, piece_values, (((0,), (0,)), ((), ())), preferr...]
    pallas_call x0 -> x8, Pallas kernels: none -> 80 us  [the longest x2 32.2 us: mesh_update(): pl.pallas_call(functools.partial(kernel, degree, place), grid=(steps,), i...]
    gather x48 -> x0, local copies, waits for them, and re-layouts: 33.2 us -> none
    dynamic_slice x65 -> x1, local copies, waits for them, and re-layouts: 23.6 us -> 0.69 us  [shards(): counts = lax.dynamic_index_in_dim(contact_counts, device, 1, keepdims=False)]
    reduce_sum x4 -> x0, other arithmetic: 20.8 us -> none  [the longest x1 12.5 us: shards(): jnp.sum(new_mesh.astype(jnp.float32).reshape(node_count, degree, features...]
    ppermute x2, waiting for transfers between devices: 0.01 us -> 14.4 us  [the longest x1 11.9 us: shards(): lax.ppermute(rims[HALO:], 'dom', [(i, i + 1) for i in range(size - 1)])]
    reshape x3 -> x4, local copies, waits for them, and re-layouts: 12.8 us -> 2.6 us  [the longest x1 0.69 us: shards(): partner_rows.reshape(-1, W)]
    convert_element_type x2 -> x0, other arithmetic: 10.2 us -> none  [the longest x1 10 us: shards(): (mesh_edges.astype(jnp.float32) + mesh_update).astype(jnp.bfloat16)]
  transfers between devices with their start and end apart: 4 -> 4, of which waited for: 1 -> 2; matrix products, arithmetic and copies ran while one was open for 50% -> 3% of each run, Pallas kernels for 0% -> 40%
where the time goes in v1:
time: 130 us
  Pallas kernels  80 us (62%)
  starting transfers between devices  26.7 us (21%)
  waiting for transfers between devices  14.4 us (11%)
  local copies, waits for them, and re-layouts  7.68 us (6%)
    pallas_call x2, Pallas kernels, mesh_update(): pl.pallas_call(functools.partial(kernel, degree, place), grid=(steps,), i...  32.2 us
    ppermute x1, waiting for transfers between devices, shards(): lax.ppermute(rims[HALO:], 'dom', [(i, i + 1) for i in range(size - 1)])  11.9 us
    pallas_call x1, Pallas kernels, contact_rest(): pl.pallas_call(functools.partial(contact_kernel, capacity), grid_spec=plt...  11.5 us
    all_to_all x1, starting transfers between devices, shards(): lax.all_to_all(outgoing, axes, split_axis=0, concat_axis=0, tiled=True)  11.5 us
    all_to_all x1, starting transfers between devices, shards(): lax.all_to_all(message.reshape(peers, capacity, W), axes, split_axis=0, c...  9.76 us
    pallas_call x1, Pallas kernels, node_update(): pl.pallas_call(node_kernel, grid=(rows.shape[0] // step,), in_specs=[pl.B...  9.73 us
    pallas_call x1, Pallas kernels, partner_part(): pl.pallas_call(functools.partial(partner_kernel, peers), grid=(count // p...  9.4 us
    pallas_call x1, Pallas kernels, received_sum(): pl.pallas_call(received_kernel, grid=(rows.shape[0] // step,), in_specs=[...  7.57 us
  transfers between devices with their start and end apart: 4, of which 2 were waited for; matrix products, arithmetic and copies ran while one was open for 3% of the time, Pallas kernels for 40%

profile of v1, /device:TPU:1, one launch (start us, length us, event | category | flops | bytes accessed | tf_op | source)
XLA Modules:
  0.0 129.6 jit_solution(13532984378865257353)
XLA Ops:
  0.6 0.0 copy-start
  0.6 7.4 %shard_map.184 = bf16[8192,128]{1,0:T(8,128)(2,1)} custom-call(s32[64,128]{1,0:T(8,128)} %bitcast.15, bf16[2048,128]{1,0:T(8,128)(2,1)} %nodes_ref.11), custom_call_target="tpu_custom_call" | custom-call | flops 4294967296 | bytes 2097152 | tf_op jit(solution)/shard_map/pallas_call | solution.py:125
  8.1 0.0 copy-start.5
  8.1 11.5 %all-to-all-start = ((bf16[128,64,128]{2,1,0:T(8,128)(2,1)}), bf16[128,64,128]{2,1,0:T(8,128)(2,1)S(1)}, u32[]{:S(2)}, u32[]{:S(2)}) async-start(bf16[128,64,128]{2,1,0:T(8,128)(2,1)} %bitcast.13), calls=%async_computation | async-start | bytes 4194304 | tf_op jit(solution)/shard_map/all_to_all | solution.py:462
  19.6 0.0 copy-done.5
  19.6 0.6 reshape.40.source_ref
  20.2 0.0 copy-done
  20.2 0.7 dynamic-slice_reduce_fusion.counts_ref
  20.9 23.1 %shard_map.186 = (bf16[12288,128]{1,0:T(8,128)(2,1)}, bf16[2048,128]{1,0:T(8,128)(2,1)}) custom-call(s32[16,6,128]{2,1,0:T(8,128)} %reshape.40.source_ref, bf16[12288,128]{1,0:T(8,128)(2,1)} %edges_ref.3, bf16[2048,128]{1,0:T(8,128)(2,1)} %nodes_ref.11, bf16[384,128]{1,0:T(8,128)(2,1)} %first_ref.8, bf16[128,128]{1,0:T(8,128)(2,1)} %second_ref.6, ...), custom_call_target="tpu_custom_call" | custom-call | flops 4246732800 | bytes 4718592 | tf_op jit(solution)/shard_map/pallas_call | solution.py:407
  44.1 9.4 %shard_map.185.part_ref = f32[8192,128]{1,0:T(8,128)} custom-call(s32[64,128]{1,0:T(8,128)} %bitcast.14, bf16[2048,128]{1,0:T(8,128)(2,1)} %nodes_ref.11, bf16[8192,128]{1,0:T(8,128)(2,1)} %bitcast.10, bf16[384,128]{1,0:T(8,128)(2,1)} %first_ref.7), custom_call_target="tpu_custom_call" | custom-call | flops 4831838208 | bytes 8388608 | tf_op jit(solution)/shard_map/pallas_call | solution.py:165
  53.5 0.0 all-to-all-done
  53.5 0.0 copy-start.1
  53.5 1.4 %copy-done.1 = bf16[128,64,128]{2,1,0:T(8,128)(2,1)} copy-done((bf16[128,64,128]{2,1,0:T(8,128)(2,1)}, bf16[128,64,128]{2,1,0:T(8,128)(2,1)S(1)}, u32[]{:S(2)}) %copy-start.1) | copy-done | bytes 2097176
  54.9 11.5 %shard_map.187 = (bf16[8192,128]{1,0:T(8,128)(2,1)}, bf16[8192,128]{1,0:T(8,128)(2,1)}) custom-call(s32[128]{0:T(128)} %dynamic-slice_reduce_fusion.counts_ref, bf16[8192,128]{1,0:T(8,128)(2,1)} %bitcast.9, f32[8192,128]{1,0:T(8,128)} %shard_map.185.part_ref, bf16[8192,128]{1,0:T(8,128)(2,1)} %bitcast.11, bf16[384,128]{1,0:T(8,128)(2,1)} %first_ref.7, ...), custom_call_target="tpu_custom_call" | custom-call | flops 1073741824 | bytes 12582912 | tf_op jit(solution)/shard_map/pallas_call | solution.py:215
  66.4 0.0 copy-start.8
  66.4 0.0 copy-start.6
  66.4 0.0 copy-start.7
  66.4 9.8 %all-to-all-start.1 = ((bf16[128,64,128]{2,1,0:T(8,128)(2,1)}), bf16[128,64,128]{2,1,0:T(8,128)(2,1)S(1)}, u32[]{:S(2)}, u32[]{:S(2)}) async-start(bf16[128,64,128]{2,1,0:T(8,128)(2,1)} %bitcast.8), calls=%async_computation.1 | async-start | bytes 4194304 | tf_op jit(solution)/shard_map/all_to_all | solution.py:482
  76.2 0.0 copy-done.8
  76.2 0.6 reshape.44.rows_ref
  76.8 2.2 %shard_map.189 = bf16[512,128]{1,0:T(8,128)(2,1)} custom-call(s32[4,128]{1,0:T(4,128)} %reshape.44.rows_ref, bf16[2048,128]{1,0:T(8,128)(2,1)} %nodes_ref.11), custom_call_target="tpu_custom_call" | custom-call | flops 268435456 | bytes 655360 | tf_op jit(solution)/shard_map/pallas_call | solution.py:145
  79.0 0.9 fusion
  79.8 3.5 %collective-permute-start = (bf16[256,128]{1,0:T(8,128)(2,1)S(1)}, bf16[256,128]{1,0:T(8,128)(2,1)S(1)}, u32[]{:S(2)}, u32[]{:S(2)}) collective-permute-start(bf16[256,128]{1,0:T(8,128)(2,1)S(1)} %get-tuple-element.16), channel_id=1, source_target_pairs={{0,1},{1,2},{2,3},{3,4},{4,5},{5,6},{6,7},{7,8},{8,9},{9,10},{10,1... | collective-permute-start | bytes 196616 | tf_op jit(solution)/shard_map/ppermute | solution.py:487
  83.4 1.9 %collective-permute-start.1 = (bf16[256,128]{1,0:T(8,128)(2,1)S(1)}, bf16[256,128]{1,0:T(8,128)(2,1)S(1)}, u32[]{:S(2)}, u32[]{:S(2)}) collective-permute-start(bf16[256,128]{1,0:T(8,128)(2,1)S(1)} %get-tuple-element.15), channel_id=1, source_target_pairs={{1,0},{2,1},{3,2},{4,3},{5,4},{6,5},{7,6},{8,7},{9,8},{10,9},{11,1... | collective-permute-start | bytes 196616 | tf_op jit(solution)/shard_map/ppermute | solution.py:488
  85.3 0.0 copy-done.6
  85.3 0.1 copy.25
  85.4 0.0 copy-done.7
  85.4 0.1 copy.24
  85.5 0.7 reshape.43.rows_ref
  86.2 0.7 reshape.36.rows_ref
  86.9 11.9 %collective-permute-done.lower_ref = bf16[256,128]{1,0:T(8,128)(2,1)S(1)} collective-permute-done((bf16[256,128]{1,0:T(8,128)(2,1)S(1)}, bf16[256,128]{1,0:T(8,128)(2,1)S(1)}, u32[]{:S(2)}, u32[]{:S(2)}) %collective-permute-start) | collective-permute-done | bytes 65568 | tf_op jit(solution)/shard_map/ppermute | solution.py:487
  98.8 0.0 copy-start.3
  98.8 2.5 %collective-permute-done.1.upper_ref = bf16[256,128]{1,0:T(8,128)(2,1)S(1)} collective-permute-done((bf16[256,128]{1,0:T(8,128)(2,1)S(1)}, bf16[256,128]{1,0:T(8,128)(2,1)S(1)}, u32[]{:S(2)}, u32[]{:S(2)}) %collective-permute-start.1) | collective-permute-done | bytes 65568 | tf_op jit(solution)/shard_map/ppermute | solution.py:488
  101.3 0.0 copy-start.4
  101.3 0.0 copy-done.3
  101.3 0.6 copy-done.4
  101.9 9.0 %shard_map.190 = (bf16[12288,128]{1,0:T(8,128)(2,1)}, bf16[2048,128]{1,0:T(8,128)(2,1)}) custom-call(s32[16,6,128]{2,1,0:T(8,128)} %reshape.40.source_ref, bf16[12288,128]{1,0:T(8,128)(2,1)} %edges_ref.3, bf16[2048,128]{1,0:T(8,128)(2,1)} %nodes_ref.11, bf16[384,128]{1,0:T(8,128)(2,1)} %first_ref.8, ...), custom_call_target="tpu_custom_call", output_to_operand_aliasing={{0}: (8, {}), {1}: (9, {})} | custom-call | flops 1415577600 | bytes 1572864 | tf_op jit(solution)/shard_map/pallas_call | solution.py:407
  111.0 7.6 %shard_map.188.received_ref = f32[1024,256]{1,0:T(8,128)} custom-call(s32[64,128]{1,0:T(8,128)} %reshape.43.rows_ref, bf16[8192,128]{1,0:T(8,128)(2,1)} %get-tuple-element.10.values_ref.after_ref), custom_call_target="tpu_custom_call" | custom-call | flops 4294967296 | bytes 2097152 | tf_op jit(solution)/shard_map/pallas_call | solution.py:264
  118.5 0.0 all-to-all-done.1
  118.5 0.0 copy-start.2
  118.5 1.3 %copy-done.2 = bf16[128,64,128]{2,1,0:T(8,128)(2,1)} copy-done((bf16[128,64,128]{2,1,0:T(8,128)(2,1)}, bf16[128,64,128]{2,1,0:T(8,128)(2,1)S(1)}, u32[]{:S(2)}) %copy-start.2) | copy-done | bytes 2097176
  119.9 9.7 %shard_map.191 = bf16[2048,128]{1,0:T(8,128)(2,1)} custom-call(s32[64,128]{1,0:T(8,128)} %reshape.36.rows_ref, bf16[8192,128]{1,0:T(8,128)(2,1)} %bitcast.12, f32[1024,256]{1,0:T(8,128)} %shard_map.188.received_ref, bf16[2048,128]{1,0:T(8,128)(2,1)} %nodes_ref.11, bf16[2048,128]{1,0:T(8,128)(2,1)} %get-tuple-element.12.mesh_ref, bf16[384,128]{1,0:T(8,128)(2,1)} %first_ref.9, ...), custom_call_target="tpu_custom_call" | custom-call | flops 4294967296 | bytes 4194304 | tf_op jit(solution)/shard_map/pallas_call | solution.py:308
Async XLA Ops:
  0.6 19.6 %copy-start = (s32[128,128]{1,0:T(8,128)S(1)}, s32[128,128]{1,0:T(8,128)}, u32[]{:S(2)}) copy-start(s32[128,128]{1,0:T(8,128)} %param.24) | copy-start | bytes 196612
  8.1 11.5 %copy-start.5 = (s32[12288]{0:T(1024)S(1)}, s32[12288]{0:T(1024)}, u32[]{:S(2)}) copy-start(s32[12288]{0:T(1024)} %param.20) | copy-start | bytes 147460
  8.1 45.4 %all-to-all-start = ((bf16[128,64,128]{2,1,0:T(8,128)(2,1)}), bf16[128,64,128]{2,1,0:T(8,128)(2,1)S(1)}, u32[]{:S(2)}, u32[]{:S(2)}) async-start(bf16[128,64,128]{2,1,0:T(8,128)(2,1)} %bitcast.13), calls=%async_computation | async-start | bytes 4194304 | tf_op jit(solution)/shard_map/all_to_all | solution.py:462
  53.5 1.4 %copy-start.1 = (bf16[128,64,128]{2,1,0:T(8,128)(2,1)}, bf16[128,64,128]{2,1,0:T(8,128)(2,1)S(1)}, u32[]{:S(2)}) copy-start(bf16[128,64,128]{2,1,0:T(8,128)(2,1)S(1)} %all-to-all-done) | copy-start | bytes 6291460
  66.4 9.8 %copy-start.8 = (s32[2,256]{1,0:T(2,128)S(1)}, s32[2,256]{1,0:T(2,128)}, u32[]{:S(2)}) copy-start(s32[2,256]{1,0:T(2,128)} %param.21) | copy-start | bytes 6148
  66.4 18.9 %copy-start.6 = (s32[128,64]{0,1:T(8,128)S(1)}, s32[128,64]{0,1:T(8,128)}, u32[]{:S(2)}) copy-start(s32[128,64]{0,1:T(8,128)} %param.23) | copy-start | bytes 98308
  66.4 19.0 %copy-start.7 = (s32[128,64]{0,1:T(8,128)S(1)}, s32[128,64]{0,1:T(8,128)}, u32[]{:S(2)}) copy-start(s32[128,64]{0,1:T(8,128)} %param.22) | copy-start | bytes 98308
  66.4 52.1 %all-to-all-start.1 = ((bf16[128,64,128]{2,1,0:T(8,128)(2,1)}), bf16[128,64,128]{2,1,0:T(8,128)(2,1)S(1)}, u32[]{:S(2)}, u32[]{:S(2)}) async-start(bf16[128,64,128]{2,1,0:T(8,128)(2,1)} %bitcast.8), calls=%async_computation.1 | async-start | bytes 4194304 | tf_op jit(solution)/shard_map/all_to_all | solution.py:482
  79.8 18.9 %collective-permute-start = (bf16[256,128]{1,0:T(8,128)(2,1)S(1)}, bf16[256,128]{1,0:T(8,128)(2,1)S(1)}, u32[]{:S(2)}, u32[]{:S(2)}) collective-permute-start(bf16[256,128]{1,0:T(8,128)(2,1)S(1)} %get-tuple-element.16), channel_id=1, source_target_pairs={{0,1},{1,2},{2,3},{3,4},{4,5},{5,6},{6,7},{7,8},{8,9},{9,10},{10,1... | collective-permute-start | bytes 196616 | tf_op jit(solution)/shard_map/ppermute | solution.py:487
  83.4 17.9 %collective-permute-start.1 = (bf16[256,128]{1,0:T(8,128)(2,1)S(1)}, bf16[256,128]{1,0:T(8,128)(2,1)S(1)}, u32[]{:S(2)}, u32[]{:S(2)}) collective-permute-start(bf16[256,128]{1,0:T(8,128)(2,1)S(1)} %get-tuple-element.15), channel_id=1, source_target_pairs={{1,0},{2,1},{3,2},{4,3},{5,4},{6,5},{7,6},{8,7},{9,8},{10,9},{11,1... | collective-permute-start | bytes 196616 | tf_op jit(solution)/shard_map/ppermute | solution.py:488
  98.8 2.6 %copy-start.3 = (bf16[256,128]{1,0:T(8,128)(2,1)}, bf16[256,128]{1,0:T(8,128)(2,1)S(1)}, u32[]{:S(2)}) copy-start(bf16[256,128]{1,0:T(8,128)(2,1)S(1)} %collective-permute-done.lower_ref) | copy-start | bytes 196612
  101.3 0.6 copy-start.4
  118.5 1.3 %copy-start.2 = (bf16[128,64,128]{2,1,0:T(8,128)(2,1)}, bf16[128,64,128]{2,1,0:T(8,128)(2,1)S(1)}, u32[]{:S(2)}) copy-start(bf16[128,64,128]{2,1,0:T(8,128)(2,1)S(1)} %all-to-all-done.1) | copy-start | bytes 6291460
